TPU v7x, 32 devices: a whole 2x2x4 slice. The times are simulated.
32 devices in a mesh: expert: 4 (over y, x), shard: 8 (over z, core).
Axes of the slice: x: 2, y: 2, z: 4, core: 2. Of those that a mesh axis runs over, the one named last changes fastest.
Arguments:
- grad_out: bfloat16 [4, 1024, 3072], P('expert', 'shard'), may hold values from -6 to 6
- gate_pre: bfloat16 [4, 1024, 8192], P('expert', None, 'shard'), may hold values from -8 to 8
- up_pre: bfloat16 [4, 1024, 8192], P('expert', None, 'shard'), may hold values from -6 to 6
- counts: int32 [4, 8], P('expert', 'shard'), may hold values from 32 to 128
- placement: int32 [4], replicated, may hold values from 0 to 63, as said below
- master: float32 [4, 8192, 3072], P('expert', 'shard')
Outputs:
- d_gate: bfloat16 [4, 1024, 8192], P('expert', None, 'shard')
- d_up: bfloat16 [4, 1024, 8192], P('expert', None, 'shard')
- new_master: float32 [4, 8192, 3072], P('expert', 'shard')
Inputs may be any that keep to these rules, and one draw needn't show every extreme that they name: `placement`: slots that hold the same expert form aligned blocks of 1, 2 or 4 consecutive slots, each block starting at a multiple of its size; different blocks hold different experts.
All inputs are finite; a program needn't handle non-finite values.
Results may differ from a plain program's by a relative error of at most 0.006.
Values may be sent and summed in bfloat16 or wider, within the bound.
No kernel may reach another device: no remote copies, remote signals or barrier semaphores. Data moves between devices by JAX's collectives and lax.ppermute only.
A program may use at most 256 MiB of HBM per device.

v0:
```python
import functools

import jax
import jax.numpy as jnp
from jax import lax
from jax.experimental import pallas as pl
from jax.experimental.pallas import tpu as pltpu
from jax.sharding import PartitionSpec as P

learn_rate = 0.02
rms_eps = 1e-06
tall = 256
params = pltpu.CompilerParams(vmem_limit_bytes=56 * 2**20)


def dot(a, b, dims):
    return lax.dot_general(a, b, (dims, ((), ())), preferred_element_type=jnp.float32)


def hidden_kernel(gate_ref, up_ref, out_ref):
    gate = gate_ref[0].astype(jnp.float32)
    hidden = gate * jax.nn.sigmoid(gate) * up_ref[0].astype(jnp.float32)
    out_ref[...] = hidden.T.astype(out_ref.dtype)


def hidden_transposed(gate_pre, up_pre):
    _, rows, ffw = gate_pre.shape
    block = pl.BlockSpec((1, tall, ffw), lambda i: (0, i, 0))
    return pl.pallas_call(
        hidden_kernel,
        grid=(rows // tall,),
        in_specs=[block, block],
        out_specs=pl.BlockSpec((ffw, tall), lambda i: (0, i)),
        out_shape=jax.ShapeDtypeStruct((ffw, rows), jnp.bfloat16),
        compiler_params=params,
    )(gate_pre, up_pre)


def update_rows(master, grads, out_ref):
    square = sum(jnp.sum(g * g, axis=1, keepdims=True) for g in grads)
    scale = learn_rate / jnp.sqrt(square / master.shape[1] + rms_eps)
    first = 0
    for grad in grads:
        cols = slice(first, first + grad.shape[1])
        out_ref[0, :, cols] = master[:, cols] - grad * scale
        first += grad.shape[1]


def gates_back(d_hidden, gate_ref, up_ref, gate_out, up_out):
    gate = gate_ref[0].astype(jnp.float32)
    up = up_ref[0].astype(jnp.float32)
    sig = jax.nn.sigmoid(gate)
    up_out[0] = (d_hidden * (gate * sig)).astype(up_out.dtype)
    slope = sig * (1.0 + gate * (1.0 - sig))
    gate_out[0] = (d_hidden * up * slope).astype(gate_out.dtype)


def phase_kernel(n_pieces, layout, wide, blocks, grad_in, gates, update, flag_ref, *refs):
    refs = list(refs)
    pieces = [refs.pop(0) for _ in range(n_pieces)]
    hidden_ref = refs.pop(0) if blocks else None
    master_hbm = refs.pop(0) if gates or update else None
    grad_ref = refs.pop(0) if grad_in else None
    gate_ref, up_ref = (refs.pop(0), refs.pop(0)) if gates else (None, None)
    gate_out, up_out = (refs.pop(0), refs.pop(0)) if gates else (None, None)
    out_ref = refs.pop(0) if blocks else None
    whole_ref, sem_ref = refs[:2]
    master_ref, master_sem = refs[2:4] if gates or update else (None, None)
    sum_ref = refs[4] if update else None
    step = pl.program_id(0)
    by_block = {}
    for place, (ref, index, row, source_first, first, count) in enumerate(layout):
        source = pieces[ref] if index is None else pieces[ref].at[index]
        high = source.shape[0]
        start = row if isinstance(row, int) else pl.multiple_of(flag_ref[row[0]], 128)
        copy = pltpu.make_async_copy(
            source.at[:, pl.ds(source_first, count)],
            whole_ref.at[pl.ds(start, high), pl.ds(first, count)],
            sem_ref.at[place],
        )
        by_block.setdefault(first // wide, []).append(copy)
    master_copies = []
    if gates or update:
        for i in range(master_ref.shape[0] // tall):
            lines = pl.ds(i * tall, tall)
            master_copies.append(
                pltpu.make_async_copy(
                    master_hbm.at[0, lines], master_ref.at[lines], master_sem.at[i]
                )
            )

    @pl.when(step == 0)
    def _():
        for block in sorted(by_block):
            for copy in by_block[block]:
                copy.start()
        for copy in master_copies:
            copy.start()

    for block in sorted(by_block):

        @pl.when(step == min(block, blocks))
        def _(block=block):
            for copy in by_block[block]:
                copy.wait()

    for i, copy in enumerate(master_copies):

        @pl.when(step == blocks + i)
        def _(copy=copy):
            copy.wait()

    if blocks:

        @pl.when(step < blocks)
        def _():
            cols = pl.ds(pl.multiple_of(step * wide, wide), wide)
            grad = dot(hidden_ref[...], whole_ref[:, cols], ((1,), (0,)))
            if grad_in:
                own = grad_ref[...].astype(jnp.float32)
                grad = own + jnp.where(flag_ref[0] > 0, grad, 0.0)
            if update:
                sum_ref[:, cols] = grad
            else:
                out_ref[...] = grad.astype(out_ref.dtype)

    if gates or update:

        @pl.when(step >= blocks)
        def _():
            lines = pl.ds(pl.multiple_of((step - blocks) * tall, tall), tall)
            if update:
                update_rows(master_ref[lines, :], [sum_ref[lines, :]], out_ref)
            if gates:
                weight = master_ref[lines, :].astype(jnp.bfloat16)
                d_hidden = dot(whole_ref[...], weight, ((1,), (1,)))
                gates_back(d_hidden, gate_ref, up_ref, gate_out, up_out)


def phase_call(flags, pieces, layout, hidden=None, master=None, grad=None, gate_up=None,
               update=False, d_model=None):
    if master is not None:
        _, ffw, d_model = master.shape
    else:
        ffw = hidden.shape[0]
    rows = gate_up[0].shape[1] if hidden is None else hidden.shape[1]
    wide = 512
    blocks = d_model // wide if hidden is not None else 0
    lines = ffw // tall if master is not None else 0
    cut = []
    for ref, index, row, first, count in layout:
        for at in range(0, count, wide):
            cut.append((ref, index, row, at, first + at, wide))
    row_block = lambda i: jnp.maximum(i - blocks, 0)
    col_block = lambda i: jnp.minimum(i, blocks - 1)
    anywhere = pl.BlockSpec(memory_space=pl.ANY)
    side = pl.BlockSpec((1, rows, tall), lambda i, flag: (0, 0, row_block(i)))
    full = pl.BlockSpec((1, tall, d_model), lambda i, flag: (0, row_block(i), 0))
    column = pl.BlockSpec((ffw, wide), lambda i, flag: (0, col_block(i)))
    specs, args = [anywhere] * len(pieces), list(pieces)
    out_specs, out_shape = [], []
    scratch = [
        pltpu.VMEM((rows, d_model), jnp.bfloat16),
        pltpu.SemaphoreType.DMA((len(cut),)),
    ]
    if hidden is not None:
        specs.append(pl.BlockSpec((ffw, rows), lambda i, flag: (0, 0)))
        args.append(hidden)
    if master is not None:
        specs.append(anywhere)
        args.append(master)
        scratch.append(pltpu.VMEM((ffw, d_model), jnp.float32))
        scratch.append(pltpu.SemaphoreType.DMA((lines,)))
    if grad is not None:
        specs.append(column)
        args.append(grad)
    if gate_up is not None:
        specs += [side, side]
        args += list(gate_up)
        out_specs += [side, side]
        out_shape += [jax.ShapeDtypeStruct(a.shape, a.dtype) for a in gate_up]
    if update:
        out_specs.append(full)
        out_shape.append(jax.ShapeDtypeStruct(master.shape, master.dtype))
        scratch.append(pltpu.VMEM((ffw, d_model), jnp.float32))
    elif hidden is not None:
        out_specs.append(column)
        out_shape.append(jax.ShapeDtypeStruct((ffw, d_model), jnp.bfloat16))
    dots = (hidden is not None) + (gate_up is not None)
    return pl.pallas_call(
        functools.partial(
            phase_kernel, len(pieces), cut, wide, blocks, grad is not None, gate_up is not None,
            update,
        ),
        grid_spec=pltpu.PrefetchScalarGridSpec(
            num_scalar_prefetch=1,
            grid=(blocks + lines,),
            in_specs=specs,
            out_specs=out_specs,
            scratch_shapes=scratch,
        ),
        out_shape=out_shape,
        compiler_params=params,
        cost_estimate=pl.CostEstimate(
            flops=2 * dots * rows * ffw * d_model,
            bytes_accessed=8 * ffw * d_model,
            transcendentals=0,
        ),
    )(flags, *args)


def update_kernel(master_ref, *refs):
    update_rows(master_ref[0], [r[...].astype(jnp.float32) for r in refs[:-1]], refs[-1])


def update_call(master, grads):
    _, ffw, d_model = master.shape
    full = pl.BlockSpec((1, 128, d_model), lambda i: (0, i, 0))
    part = pl.BlockSpec((128, grads[0].shape[1]), lambda i: (i, 0))
    return pl.pallas_call(
        update_kernel,
        grid=(ffw // 128,),
        in_specs=[full] + [part] * len(grads),
        out_specs=full,
        out_shape=jax.ShapeDtypeStruct(master.shape, master.dtype),
        compiler_params=params,
    )(master, *grads)


def after(value, other):
    return lax.optimization_barrier((value, other))[0]


def per_device(grad_out, gate_pre, up_pre, counts, placement, master):
    n_slot = lax.axis_size("expert")
    n_shard = lax.axis_size("shard")
    chips = n_shard // 2
    core = lax.axis_index("shard") % 2
    chip = lax.axis_index("shard") // 2
    slot = lax.axis_index("expert")
    rows, d_model = grad_out.shape[1:]
    order = jnp.arange(n_slot, dtype=jnp.int32)
    same = placement[:, None] == placement[None, :]
    pair_count = jnp.sum(same & (order[:, None] ^ 1 == order[None, :]), dtype=jnp.int32)
    four_count = jnp.sum(same & (order[:, None] ^ 2 == order[None, :]), dtype=jnp.int32)

    def share(bit):
        return jnp.any(same & (order[:, None] == slot) & (order[None, :] == slot ^ bit))

    def to_slot(value, bit):
        return lax.ppermute(value, "expert", [(i, i ^ bit) for i in range(n_slot)])

    def to_core(value):
        return lax.ppermute(value, "shard", [(i, i ^ 1) for i in range(n_shard)])

    def to_chip(value, pairs):
        pairs = [(2 * a + c, 2 * b + c) for a, b in pairs for c in range(2)]
        return lax.ppermute(value, "shard", pairs)

    def along_chips(block, held=None):
        if chips != 4:
            return [block] + [
                to_chip(block, [((z + far) % chips, z) for z in range(chips)])
                for far in range(1, chips)
            ]
        two = to_chip(block, [(0, 2), (1, 3), (2, 0), (3, 1)])
        one = to_chip(block, [(1, 0), (2, 1), (3, 2)])
        three = to_chip(block, [(0, 1), (1, 2), (2, 3)])
        end = to_chip(two if held is None else after(two, held), [(2, 3), (1, 0)])
        one = jnp.where(chip == 3, end, one)
        three = jnp.where(chip == 0, end, three)
        return [block, one, two, three]

    def all_sum(grad):
        half = grad.shape[0] // 2
        done = []
        for part, bits in ((grad[:half], (1, 2)), (grad[half:], (2, 1))):
            sides = [jnp.where(slot & bit > 0, 1, 0) for bit in bits]
            for bit, side in zip(bits, sides):
                high = part.shape[0] // 2
                keep = lax.dynamic_slice_in_dim(part, side * high, high)
                send = lax.dynamic_slice_in_dim(part, (1 - side) * high, high)
                got = to_slot(send, bit)
                part = (keep.astype(jnp.float32) + got.astype(jnp.float32)).astype(part.dtype)
            for bit, side in zip(bits[::-1], sides[::-1]):
                got = to_slot(part, bit)
                part = jnp.concatenate(
                    [jnp.where(side == 0, part, got), jnp.where(side == 0, got, part)]
                )
            done.append(part)
        return jnp.concatenate(done)

    def body(mode, grad_out, gate_pre, up_pre, counts, placement, master):
        live = jnp.arange(rows, dtype=jnp.int32) < counts[0, 0]
        masked = jnp.where(live[:, None], grad_out[0], jnp.zeros((), grad_out.dtype))

        def gather(block):
            return lax.all_gather(block, "shard", axis=0, tiled=True)

        gate_up = (gate_pre, up_pre)
        if mode == "pair":
            middle = d_model * 2 // 3
            early = to_slot(masked[:, :middle], 1)
            hidden = hidden_transposed(gate_pre, up_pre)
            high = hidden.shape[0] // 2
            top = to_slot(after(hidden[:high], early), 1)
            low = to_slot(after(hidden[high:], early), 1)
            mine = along_chips(masked, top)
            other = [to_core(piece) for piece in mine]
            first = along_chips(early)
            first = first + [to_core(piece) for piece in first]
            late = jnp.stack([piece[:, middle:] for piece in mine])
            late = to_slot(after(late, low), 1)
            late = [late, to_core(late)]
            theirs = jnp.concatenate([top, low])
            steps = [(chip + far) % chips for far in range(chips)]
            spots = [(2 * s + (core ^ swap)) * rows for swap in range(2) for s in steps]
            flags = jnp.stack([share(1).astype(jnp.int32)] + spots)
            layout = [(i, None, (1 + i,), 0, d_model) for i in range(n_shard)]
            d_gate, d_up, grad = phase_call(
                flags, after(mine, first[2]) + other, layout, hidden, master, gate_up=gate_up
            )
            layout = [(i, None, (1 + i,), 0, middle) for i in range(n_shard)]
            layout += [
                (n_shard + i // chips, i % chips, (1 + i,), middle, d_model - middle)
                for i in range(n_shard)
            ]
            fresh = phase_call(
                flags, first + late, layout, theirs, master, grad=grad, update=True
            )[0]
            return d_gate, d_up, fresh
        hidden = hidden_transposed(gate_pre, up_pre)
        flags = jnp.zeros((1,), jnp.int32)
        if mode == "none":
            layout = [(0, None, 0, 0, d_model)]
            return tuple(
                phase_call(
                    flags, [gather(masked)], layout, hidden, master, gate_up=gate_up, update=True
                )
            )
        half = d_model // 2
        one = gather(masked[:, :half])
        two = gather(after(masked[:, half:], one))
        layout = [(0, None, 0, 0, half)]
        grads = []
        for whole in (one, two):
            grad = phase_call(flags, [whole], layout, hidden, d_model=half)[0]
            if mode == "four":
                grad = all_sum(grad)
            else:
                for bit in (1, 2):
                    got = to_slot(grad, bit)
                    grad = grad + jnp.where(share(bit), got, jnp.zeros((), got.dtype))
            grads.append(grad)
        layout = layout + [(1, None, 0, half, half)]
        d_gate, d_up = phase_call(flags, [one, two], layout, master=master, gate_up=gate_up)
        return d_gate, d_up, update_call(master, grads)

    modes = ["none", "pair", "four"] + (["mixed"] if n_slot > 4 else [])
    mixed = jnp.where(four_count == n_slot, 2, len(modes) - 1)
    which = jnp.where(four_count > 0, mixed, jnp.where(pair_count > 0, 1, 0))
    return lax.switch(
        which,
        [lambda *a, mode=mode: body(mode, *a) for mode in modes],
        grad_out, gate_pre, up_pre, counts, placement, master,
    )


def solution(mesh):
    return jax.shard_map(
        per_device,
        mesh=mesh,
        in_specs=(
            P("expert", "shard", None),
            P("expert", None, "shard"),
            P("expert", None, "shard"),
            P("expert", "shard"),
            P(),
            P("expert", "shard", None),
        ),
        out_specs=(
            P("expert", None, "shard"),
            P("expert", None, "shard"),
            P("expert", "shard", None),
        ),
        check_vma=False,
    )
```

profile of v0, /device:TPU:0, one launch (start us, length us, event | category | flops | bytes accessed | tf_op | source)
XLA Modules:
  0.0 188.3 jit_solution(2214449733138431013)
XLA Ops:
  7.2 0.8 broadcast_compare_fusion.2
  8.0 1.4 convert_reduce_fusion
  10.7 170.7 %conditional.1 = ((bf16[1,1024,1024]{2,1,0:T(8,128)(2,1)}, bf16[1,1024,1024]{2,1,0:T(8,128)(2,1)}, f32[1,1024,3072]{2,1,0:T(8,128)})) conditional(s32[]{:T(128)} %clamp.3, (s32[1,1]{1,0:T(1,128)}, bf16[1,128,3072]{2,1,0:T(8,128)(2,1)}, bf16[1,1024,1024]{2,1,0:T(8,128)(2,1)}, bf16[1,1024,1024]{2,1,0:T(8,128)(2,1)}, ...), branch_computations={%region_2.3_spmd, %region_3.5_spmd, %region_5.6_spmd} | conditional | flops 19334823936 | bytes 226756256 | solution.py:362
  10.8 0.0 copy-start.1
  10.8 0.8 iota_compare_fusion.1
  11.6 1.3 bitcast_select_fusion.1.refs_0_
  12.9 3.0 %collective-permute-start.1 = (bf16[128,2048]{1,0:T(8,128)(2,1)S(1)}, bf16[128,2048]{1,0:T(8,128)(2,1)S(1)}, u32[]{:S(2)}, u32[]{:S(2)}) collective-permute-start(bf16[128,2048]{1,0:T(8,128)(2,1)S(1)} %slice.40), channel_id=1, source_target_pairs={{0,8},{8,0},{16,24},{24,16},{1,9},{9,1},{17,25},{25,17},{2,10},{10... | collective-permute-start | bytes 1572872 | tf_op jit(solution)/shard_map/cond/branch_1_fun/ppermute | solution.py:251
  15.9 4.3 %branch_1_fun.3.refs_8_ = bf16[1024,1024]{1,0:T(8,128)(2,1)} custom-call(bf16[1,1024,1024]{2,1,0:T(8,128)(2,1)S(1)} %copy-done.1, bf16[1,1024,1024]{2,1,0:T(8,128)(2,1)} %get-tuple-element.57.up_ref.refs_11_), custom_call_target="tpu_custom_call" | custom-call | tf_op jit(solution)/shard_map/cond/branch_1_fun/pallas_call | solution.py:29
  20.2 2.7 %fusion.2 = (bf16[512,1024]{1,0:T(8,128)(2,1)}, bf16[512,1024]{1,0:T(8,128)(2,1)S(1)}) fusion(bf16[1024,1024]{1,0:T(8,128)(2,1)} %branch_1_fun.3.refs_8_), kind=kLoop, calls=%fused_computation.66 | loop fusion | bytes 4194304 | tf_op jit(solution)/shard_map/cond/branch_1_fun/slice | solution.py:307
  22.9 4.9 %collective-permute-done.1.refs_0_ = bf16[128,2048]{1,0:T(8,128)(2,1)S(1)} collective-permute-done((bf16[128,2048]{1,0:T(8,128)(2,1)S(1)}, bf16[128,2048]{1,0:T(8,128)(2,1)S(1)}, u32[]{:S(2)}, u32[]{:S(2)}) %collective-permute-start.1) | collective-permute-done | bytes 524320 | tf_op jit(solution)/shard_map/cond/branch_1_fun/ppermute | solution.py:251
  27.8 1.7 collective-permute-start.2
  29.6 2.6 %collective-permute-start = (bf16[128,3072]{1,0:T(8,128)(2,1)S(1)}, bf16[128,3072]{1,0:T(8,128)(2,1)}, u32[]{:S(2)}, u32[]{:S(2)}) collective-permute-start(bf16[128,3072]{1,0:T(8,128)(2,1)S(1)} %bitcast_select_fusion.1.refs_0_), channel_id=1, source_target_pairs={{0,4},{1,5},{2,6},{3,7},{4,0},{5,1},{6,2},{7,3},{8,12},{9,13},{10,... | collective-permute-start | bytes 2359304 | tf_op jit(solution)/shard_map/cond/branch_1_fun/ppermute | solution.py:258
  32.1 4.4 %collective-permute-start.5 = (bf16[128,3072]{1,0:T(8,128)(2,1)S(1)}, bf16[128,3072]{1,0:T(8,128)(2,1)}, u32[]{:S(2)}, u32[]{:S(2)}) collective-permute-start(bf16[128,3072]{1,0:T(8,128)(2,1)S(1)} %bitcast_select_fusion.1.refs_0_), channel_id=1, source_target_pairs={{0,2},{1,3},{2,4},{3,5},{4,6},{5,7},{8,10},{9,11},{10,12},{11,13},... | collective-permute-start | bytes 2359304 | tf_op jit(solution)/shard_map/cond/branch_1_fun/ppermute | solution.py:258
  36.5 1.3 collective-permute-start.4
  37.8 29.0 %collective-permute-done.refs_2_ = bf16[128,3072]{1,0:T(8,128)(2,1)} collective-permute-done((bf16[128,3072]{1,0:T(8,128)(2,1)S(1)}, bf16[128,3072]{1,0:T(8,128)(2,1)}, u32[]{:S(2)}, u32[]{:S(2)}) %collective-permute-start) | collective-permute-done | bytes 786464 | tf_op jit(solution)/shard_map/cond/branch_1_fun/ppermute | solution.py:258
  66.8 1.3 collective-permute-start.3
  68.1 4.5 %collective-permute-start.6 = (bf16[128,2048]{1,0:T(8,128)(2,1)S(1)}, bf16[128,2048]{1,0:T(8,128)(2,1)}, u32[]{:S(2)}, u32[]{:S(2)}) collective-permute-start(bf16[128,2048]{1,0:T(8,128)(2,1)S(1)} %collective-permute-done.1.refs_0_), channel_id=1, source_target_pairs={{0,4},{1,5},{2,6},{3,7},{4,0},{5,1},{6,2},{7,3},{8,12},{9,13},{10,... | collective-permute-start | bytes 1572872 | tf_op jit(solution)/shard_map/cond/branch_1_fun/ppermute | solution.py:258
  72.6 0.6 collective-permute-start.18
  73.2 1.0 slice_bitcast_fusion.1
  74.1 22.9 %collective-permute-start.13 = (bf16[128,2048]{1,0:T(8,128)(2,1)S(1)}, bf16[128,2048]{1,0:T(8,128)(2,1)}, u32[]{:S(2)}, u32[]{:S(2)}) collective-permute-start(bf16[128,2048]{1,0:T(8,128)(2,1)S(1)} %collective-permute-done.1.refs_0_), channel_id=1, source_target_pairs={{0,2},{1,3},{2,4},{3,5},{4,6},{5,7},{8,10},{9,11},{10,12},{11,13},... | collective-permute-start | bytes 1572872 | tf_op jit(solution)/shard_map/cond/branch_1_fun/ppermute | solution.py:258
  97.1 0.0 collective-permute-done.4
  97.1 1.3 collective-permute-start.12
  98.4 7.8 %collective-permute-done.6.refs_2_ = bf16[128,2048]{1,0:T(8,128)(2,1)} collective-permute-done((bf16[128,2048]{1,0:T(8,128)(2,1)S(1)}, bf16[128,2048]{1,0:T(8,128)(2,1)}, u32[]{:S(2)}, u32[]{:S(2)}) %collective-permute-start.6) | collective-permute-done | bytes 524320 | tf_op jit(solution)/shard_map/cond/branch_1_fun/ppermute | solution.py:258
  106.1 1.5 collective-permute-start.11
  107.6 0.0 collective-permute-done.3
  107.6 1.5 broadcast_select_fusion
  109.2 1.3 pad_maximum_fusion.1
  110.5 0.0 collective-permute-done.18
  110.5 0.6 collective-permute-start.19
  111.1 0.4 copy-done.17
  111.5 0.6 collective-permute-start.9
  112.1 4.1 %collective-permute-done.12 = bf16[128,2048]{1,0:T(8,128)(2,1)} collective-permute-done((bf16[128,2048]{1,0:T(8,128)(2,1)S(1)}, bf16[128,2048]{1,0:T(8,128)(2,1)}, u32[]{:S(2)}, u32[]{:S(2)}) %collective-permute-start.12) | collective-permute-done | bytes 524320 | tf_op jit(solution)/shard_map/cond/branch_1_fun/ppermute | solution.py:258
  116.2 11.1 %collective-permute-done.11 = bf16[128,2048]{1,0:T(8,128)(2,1)} collective-permute-done((bf16[128,2048]{1,0:T(8,128)(2,1)}, bf16[128,2048]{1,0:T(8,128)(2,1)}, u32[]{:S(2)}, u32[]{:S(2)}) %collective-permute-start.11) | collective-permute-done | bytes 524320 | tf_op jit(solution)/shard_map/cond/branch_1_fun/ppermute | solution.py:258
  127.4 0.0 collective-permute-start.8
  127.4 0.8 and_reduce_fusion
  128.8 0.6 stack.42.flag_ref
  129.4 3.1 %pad_maximum_fusion.refs_10_ = bf16[1024,1024]{1,0:T(8,128)(2,1)} fusion(bf16[512,1024]{1,0:T(8,128)(2,1)} %copy-done.17, bf16[512,1024]{1,0:T(8,128)(2,1)} %collective-permute-done.2), kind=kLoop, calls=%fused_computation.2 | loop fusion | flops 4194304 | bytes 4194304 | tf_op jit(solution)/shard_map/cond/branch_1_fun/concatenate | solution.py:315
  132.5 1.4 broadcast_select_fusion.2
  134.0 0.6 collective-permute-start.14
  134.6 0.1 collective-permute-start.16
  134.7 0.4 collective-permute-start.17
  135.1 0.1 collective-permute-start.15
  135.2 0.4 collective-permute-start.20
  135.6 22.6 %branch_1_fun.4 = (bf16[1,1024,1024]{2,1,0:T(8,128)(2,1)}, bf16[1,1024,1024]{2,1,0:T(8,128)(2,1)}, bf16[1024,3072]{1,0:T(8,128)(2,1)}) custom-call(s32[9]{0:T(128)} %stack.42.flag_ref, bf16[128,3072]{1,0:T(8,128)(2,1)} %copy-done.9, bf16[128,3072]{1,0:T(8,128)(2,1)} %copy-done.16, bf16[128,3072]{1,0:T(8,128)(2,1)} %collective-permute-done.refs_2_, ...), custom_call_target="tpu_custom_call" | custom-call | flops 12884901888 | bytes 25165824 | tf_op jit(solution)/shard_map/cond/branch_1_fun/pallas_call | solution.py:190
  158.3 0.7 copy-done.20
  159.0 0.2 copy-done.21
  159.2 0.3 copy-done.18
  159.6 21.4 %branch_1_fun.5 = f32[1,1024,3072]{2,1,0:T(8,128)} custom-call(s32[9]{0:T(128)} %stack.42.flag_ref, bf16[128,2048]{1,0:T(8,128)(2,1)} %copy-done.19, bf16[128,2048]{1,0:T(8,128)(2,1)} %copy-done.13, bf16[128,2048]{1,0:T(8,128)(2,1)} %collective-permute-done.6.refs_2_, bf16[128,2048]{1,0:T(8,128)(2,1)} %copy-done.12, bf16[128,2048]{1,0:T(8,128)(2,1)} %copy-done.20, ...), custom_call_target="tpu_custom_call" | custom-call | flops 6442450944 | bytes 25165824 | tf_op jit(solution)/shard_map/cond/branch_1_fun/pallas_call | solution.py:190
  (40 shorter events, 0.2 us)
Async XLA Ops:
  10.8 5.1 %copy-start.1 = (bf16[1,1024,1024]{2,1,0:T(8,128)(2,1)S(1)}, bf16[1,1024,1024]{2,1,0:T(8,128)(2,1)}, u32[]{:S(2)}) copy-start(bf16[1,1024,1024]{2,1,0:T(8,128)(2,1)} %get-tuple-element.56.gate_ref.refs_10_) | copy-start | bytes 6291460 | tf_op jit(solution)/shard_map/cond
  12.8 98.3 %copy-start.9 = (bf16[128,3072]{1,0:T(8,128)(2,1)}, bf16[128,3072]{1,0:T(8,128)(2,1)S(1)}, u32[]{:S(2)}) copy-start(bf16[128,3072]{1,0:T(8,128)(2,1)S(1)} %bitcast_select_fusion.1.refs_0_) | copy-start | bytes 2359300 | tf_op jit(solution)/shard_map/cond
  12.9 14.9 %collective-permute-start.1 = (bf16[128,2048]{1,0:T(8,128)(2,1)S(1)}, bf16[128,2048]{1,0:T(8,128)(2,1)S(1)}, u32[]{:S(2)}, u32[]{:S(2)}) collective-permute-start(bf16[128,2048]{1,0:T(8,128)(2,1)S(1)} %slice.40), channel_id=1, source_target_pairs={{0,8},{8,0},{16,24},{24,16},{1,9},{9,1},{17,25},{25,17},{2,10},{10... | collective-permute-start | bytes 1572872 | tf_op jit(solution)/shard_map/cond/branch_1_fun/ppermute | solution.py:251
  27.8 106.2 %copy-start.19 = (bf16[128,2048]{1,0:T(8,128)(2,1)}, bf16[128,2048]{1,0:T(8,128)(2,1)S(1)}, u32[]{:S(2)}) copy-start(bf16[128,2048]{1,0:T(8,128)(2,1)S(1)} %collective-permute-done.1.refs_0_) | copy-start | bytes 1572868 | tf_op jit(solution)/shard_map/cond
  27.8 39.0 %collective-permute-start.2 = (bf16[512,1024]{1,0:T(8,128)(2,1)S(1)}, bf16[512,1024]{1,0:T(8,128)(2,1)}, u32[]{:S(2)}, u32[]{:S(2)}) collective-permute-start(bf16[512,1024]{1,0:T(8,128)(2,1)S(1)} %get-tuple-element.58), channel_id=1, source_target_pairs={{0,8},{8,0},{16,24},{24,16},{1,9},{9,1},{17,25},{25,17},{2,10},{10... | collective-permute-start | bytes 3145736 | tf_op jit(solution)/shard_map/cond/branch_1_fun/ppermute | solution.py:251
  29.6 37.2 %collective-permute-start = (bf16[128,3072]{1,0:T(8,128)(2,1)S(1)}, bf16[128,3072]{1,0:T(8,128)(2,1)}, u32[]{:S(2)}, u32[]{:S(2)}) collective-permute-start(bf16[128,3072]{1,0:T(8,128)(2,1)S(1)} %bitcast_select_fusion.1.refs_0_), channel_id=1, source_target_pairs={{0,4},{1,5},{2,6},{3,7},{4,0},{5,1},{6,2},{7,3},{8,12},{9,13},{10,... | collective-permute-start | bytes 2359304 | tf_op jit(solution)/shard_map/cond/branch_1_fun/ppermute | solution.py:258
  32.1 42.0 %collective-permute-start.5 = (bf16[128,3072]{1,0:T(8,128)(2,1)S(1)}, bf16[128,3072]{1,0:T(8,128)(2,1)}, u32[]{:S(2)}, u32[]{:S(2)}) collective-permute-start(bf16[128,3072]{1,0:T(8,128)(2,1)S(1)} %bitcast_select_fusion.1.refs_0_), channel_id=1, source_target_pairs={{0,2},{1,3},{2,4},{3,5},{4,6},{5,7},{8,10},{9,11},{10,12},{11,13},... | collective-permute-start | bytes 2359304 | tf_op jit(solution)/shard_map/cond/branch_1_fun/ppermute | solution.py:258
  36.5 60.6 %collective-permute-start.4 = (bf16[128,3072]{1,0:T(8,128)(2,1)S(1)}, bf16[128,3072]{1,0:T(8,128)(2,1)}, u32[]{:S(2)}, u32[]{:S(2)}) collective-permute-start(bf16[128,3072]{1,0:T(8,128)(2,1)S(1)} %bitcast_select_fusion.1.refs_0_), channel_id=1, source_target_pairs={{2,0},{3,1},{4,2},{5,3},{6,4},{7,5},{10,8},{11,9},{12,10},{13,11},... | collective-permute-start | bytes 2359304 | tf_op jit(solution)/shard_map/cond/branch_1_fun/ppermute | solution.py:258
  66.8 40.8 %collective-permute-start.3 = (bf16[128,3072]{1,0:T(8,128)(2,1)}, bf16[128,3072]{1,0:T(8,128)(2,1)}, u32[]{:S(2)}, u32[]{:S(2)}) collective-permute-start(bf16[128,3072]{1,0:T(8,128)(2,1)} %collective-permute-done.refs_2_), channel_id=1, source_target_pairs={{4,6},{5,7},{2,0},{3,1},{12,14},{13,15},{10,8},{11,9},{20,22},{21,... | collective-permute-start | bytes 2359304 | tf_op jit(solution)/shard_map/cond/branch_1_fun/ppermute | solution.py:258
  68.1 38.1 %collective-permute-start.6 = (bf16[128,2048]{1,0:T(8,128)(2,1)S(1)}, bf16[128,2048]{1,0:T(8,128)(2,1)}, u32[]{:S(2)}, u32[]{:S(2)}) collective-permute-start(bf16[128,2048]{1,0:T(8,128)(2,1)S(1)} %collective-permute-done.1.refs_0_), channel_id=1, source_target_pairs={{0,4},{1,5},{2,6},{3,7},{4,0},{5,1},{6,2},{7,3},{8,12},{9,13},{10,... | collective-permute-start | bytes 1572872 | tf_op jit(solution)/shard_map/cond/branch_1_fun/ppermute | solution.py:258
  72.6 38.0 %collective-permute-start.18 = (bf16[512,1024]{1,0:T(8,128)(2,1)}, bf16[512,1024]{1,0:T(8,128)(2,1)S(1)}, u32[]{:S(2)}, u32[]{:S(2)}) collective-permute-start(bf16[512,1024]{1,0:T(8,128)(2,1)} %get-tuple-element.67), channel_id=1, source_target_pairs={{0,8},{8,0},{16,24},{24,16},{1,9},{9,1},{17,25},{25,17},{2,10},{10... | collective-permute-start | bytes 3145736 | tf_op jit(solution)/shard_map/cond/branch_1_fun/ppermute | solution.py:251
  74.1 37.4 %collective-permute-start.13 = (bf16[128,2048]{1,0:T(8,128)(2,1)S(1)}, bf16[128,2048]{1,0:T(8,128)(2,1)}, u32[]{:S(2)}, u32[]{:S(2)}) collective-permute-start(bf16[128,2048]{1,0:T(8,128)(2,1)S(1)} %collective-permute-done.1.refs_0_), channel_id=1, source_target_pairs={{0,2},{1,3},{2,4},{3,5},{4,6},{5,7},{8,10},{9,11},{10,12},{11,13},... | collective-permute-start | bytes 1572872 | tf_op jit(solution)/shard_map/cond/branch_1_fun/ppermute | solution.py:258
  97.1 19.2 %collective-permute-start.12 = (bf16[128,2048]{1,0:T(8,128)(2,1)S(1)}, bf16[128,2048]{1,0:T(8,128)(2,1)}, u32[]{:S(2)}, u32[]{:S(2)}) collective-permute-start(bf16[128,2048]{1,0:T(8,128)(2,1)S(1)} %collective-permute-done.1.refs_0_), channel_id=1, source_target_pairs={{2,0},{3,1},{4,2},{5,3},{6,4},{7,5},{10,8},{11,9},{12,10},{13,11},... | collective-permute-start | bytes 1572872 | tf_op jit(solution)/shard_map/cond/branch_1_fun/ppermute | solution.py:258
  106.1 21.3 %collective-permute-start.11 = (bf16[128,2048]{1,0:T(8,128)(2,1)}, bf16[128,2048]{1,0:T(8,128)(2,1)}, u32[]{:S(2)}, u32[]{:S(2)}) collective-permute-start(bf16[128,2048]{1,0:T(8,128)(2,1)} %collective-permute-done.6.refs_2_), channel_id=1, source_target_pairs={{4,6},{5,7},{2,0},{3,1},{12,14},{13,15},{10,8},{11,9},{20,22},{21,... | collective-permute-start | bytes 1572872 | tf_op jit(solution)/shard_map/cond/branch_1_fun/ppermute | solution.py:258
  109.1 1.4 copy-start.15
  109.1 2.0 %copy-start.16 = (bf16[128,3072]{1,0:T(8,128)(2,1)}, bf16[128,3072]{1,0:T(8,128)(2,1)S(1)}, u32[]{:S(2)}) copy-start(bf16[128,3072]{1,0:T(8,128)(2,1)S(1)} %get-tuple-element.61.refs_1_) | copy-start | bytes 2359300 | tf_op jit(solution)/shard_map/cond
  110.5 1.0 copy-start.17
  110.5 24.7 %collective-permute-start.19 = (bf16[4,128,1024]{2,1,0:T(8,128)(2,1)}, bf16[4,128,1024]{2,1,0:T(8,128)(2,1)}, u32[]{:S(2)}, u32[]{:S(2)}) collective-permute-start(bf16[4,128,1024]{2,1,0:T(8,128)(2,1)} %pad_maximum_fusion.1), channel_id=1, source_target_pairs={{0,8},{8,0},{16,24},{24,16},{1,9},{9,1},{17,25},{25,17},{2,10},{10... | collective-permute-start | bytes 3145736 | tf_op jit(solution)/shard_map/cond/branch_1_fun/ppermute | solution.py:251
  111.5 22.5 %collective-permute-start.7 = (bf16[128,3072]{1,0:T(8,128)(2,1)S(1)}, bf16[128,3072]{1,0:T(8,128)(2,1)}, u32[]{:S(2)}, u32[]{:S(2)}) collective-permute-start(bf16[128,3072]{1,0:T(8,128)(2,1)S(1)} %bitcast_select_fusion.1.refs_0_), channel_id=1, source_target_pairs={{0,1},{1,0},{2,3},{3,2},{4,5},{5,4},{6,7},{7,6},{8,9},{9,8},{10,11... | collective-permute-start | bytes 2359304 | tf_op jit(solution)/shard_map/cond/branch_1_fun/ppermute | solution.py:254
  111.5 23.1 %collective-permute-start.9 = (bf16[128,3072]{1,0:T(8,128)(2,1)}, bf16[128,3072]{1,0:T(8,128)(2,1)}, u32[]{:S(2)}, u32[]{:S(2)}) collective-permute-start(bf16[128,3072]{1,0:T(8,128)(2,1)} %collective-permute-done.refs_2_), channel_id=1, source_target_pairs={{0,1},{1,0},{2,3},{3,2},{4,5},{5,4},{6,7},{7,6},{8,9},{9,8},{10,11... | collective-permute-start | bytes 2359304 | tf_op jit(solution)/shard_map/cond/branch_1_fun/ppermute | solution.py:254
  116.2 18.4 %collective-permute-start.10 = (bf16[128,3072]{1,0:T(8,128)(2,1)}, bf16[128,3072]{1,0:T(8,128)(2,1)}, u32[]{:S(2)}, u32[]{:S(2)}) collective-permute-start(bf16[128,3072]{1,0:T(8,128)(2,1)} %copy-done.15), channel_id=1, source_target_pairs={{0,1},{1,0},{2,3},{3,2},{4,5},{5,4},{6,7},{7,6},{8,9},{9,8},{10,11... | collective-permute-start | bytes 2359304 | tf_op jit(solution)/shard_map/cond/branch_1_fun/ppermute | solution.py:254
  127.4 7.7 %collective-permute-start.8 = (bf16[128,3072]{1,0:T(8,128)(2,1)}, bf16[128,3072]{1,0:T(8,128)(2,1)}, u32[]{:S(2)}, u32[]{:S(2)}) collective-permute-start(bf16[128,3072]{1,0:T(8,128)(2,1)} %copy-done.16), channel_id=1, source_target_pairs={{0,1},{1,0},{2,3},{3,2},{4,5},{5,4},{6,7},{7,6},{8,9},{9,8},{10,11... | collective-permute-start | bytes 2359304 | tf_op jit(solution)/shard_map/cond/branch_1_fun/ppermute | solution.py:254
  132.5 3.1 %copy-start.3 = (bf16[1,1024,1024]{2,1,0:T(8,128)(2,1)S(1)}, bf16[1,1024,1024]{2,1,0:T(8,128)(2,1)}, u32[]{:S(2)}) copy-start(bf16[1,1024,1024]{2,1,0:T(8,128)(2,1)} %get-tuple-element.57.up_ref.refs_11_) | copy-start | bytes 6291460 | tf_op jit(solution)/shard_map/cond
  134.0 24.2 %copy-start.12 = (bf16[128,2048]{1,0:T(8,128)(2,1)}, bf16[128,2048]{1,0:T(8,128)(2,1)S(1)}, u32[]{:S(2)}) copy-start(bf16[128,2048]{1,0:T(8,128)(2,1)S(1)} %get-tuple-element.119.refs_3_) | copy-start | bytes 1572868 | tf_op jit(solution)/shard_map/cond
  134.0 24.2 %copy-start.13 = (bf16[128,2048]{1,0:T(8,128)(2,1)}, bf16[128,2048]{1,0:T(8,128)(2,1)S(1)}, u32[]{:S(2)}) copy-start(bf16[128,2048]{1,0:T(8,128)(2,1)S(1)} %get-tuple-element.120.refs_1_) | copy-start | bytes 1572868 | tf_op jit(solution)/shard_map/cond
  134.0 24.2 %collective-permute-start.14 = (bf16[128,2048]{1,0:T(8,128)(2,1)S(1)}, bf16[128,2048]{1,0:T(8,128)(2,1)S(1)}, u32[]{:S(2)}, u32[]{:S(2)}) collective-permute-start(bf16[128,2048]{1,0:T(8,128)(2,1)S(1)} %collective-permute-done.1.refs_0_), channel_id=1, source_target_pairs={{0,1},{1,0},{2,3},{3,2},{4,5},{5,4},{6,7},{7,6},{8,9},{9,8},{10,11... | collective-permute-start | bytes 1572872 | tf_op jit(solution)/shard_map/cond/branch_1_fun/ppermute | solution.py:254
  134.6 23.7 %collective-permute-start.16 = (bf16[128,2048]{1,0:T(8,128)(2,1)}, bf16[128,2048]{1,0:T(8,128)(2,1)S(1)}, u32[]{:S(2)}, u32[]{:S(2)}) collective-permute-start(bf16[128,2048]{1,0:T(8,128)(2,1)} %collective-permute-done.6.refs_2_), channel_id=1, source_target_pairs={{0,1},{1,0},{2,3},{3,2},{4,5},{5,4},{6,7},{7,6},{8,9},{9,8},{10,11... | collective-permute-start | bytes 1572872 | tf_op jit(solution)/shard_map/cond/branch_1_fun/ppermute | solution.py:254
  134.7 23.6 %collective-permute-start.17 = (bf16[128,2048]{1,0:T(8,128)(2,1)S(1)}, bf16[128,2048]{1,0:T(8,128)(2,1)}, u32[]{:S(2)}, u32[]{:S(2)}) collective-permute-start(bf16[128,2048]{1,0:T(8,128)(2,1)S(1)} %get-tuple-element.119.refs_3_), channel_id=1, source_target_pairs={{0,1},{1,0},{2,3},{3,2},{4,5},{5,4},{6,7},{7,6},{8,9},{9,8},{10,11... | collective-permute-start | bytes 1572872 | tf_op jit(solution)/shard_map/cond/branch_1_fun/ppermute | solution.py:254
  135.1 23.2 %collective-permute-start.15 = (bf16[128,2048]{1,0:T(8,128)(2,1)S(1)}, bf16[128,2048]{1,0:T(8,128)(2,1)}, u32[]{:S(2)}, u32[]{:S(2)}) collective-permute-start(bf16[128,2048]{1,0:T(8,128)(2,1)S(1)} %get-tuple-element.120.refs_1_), channel_id=1, source_target_pairs={{0,1},{1,0},{2,3},{3,2},{4,5},{5,4},{6,7},{7,6},{8,9},{9,8},{10,11... | collective-permute-start | bytes 1572872 | tf_op jit(solution)/shard_map/cond/branch_1_fun/ppermute | solution.py:254
  135.2 23.1 %collective-permute-start.20 = (bf16[4,128,1024]{2,1,0:T(8,128)(2,1)}, bf16[4,128,1024]{2,1,0:T(8,128)(2,1)S(1)}, u32[]{:S(2)}, u32[]{:S(2)}) collective-permute-start(bf16[4,128,1024]{2,1,0:T(8,128)(2,1)} %collective-permute-done.19.refs_8_), channel_id=1, source_target_pairs={{0,1},{1,0},{2,3},{3,2},{4,5},{5,4},{6,7},{7,6},{8,9},{9,8},{10,11... | collective-permute-start | bytes 3145736 | tf_op jit(solution)/shard_map/cond/branch_1_fun/ppermute | solution.py:254
  158.2 0.8 copy-start.20
  158.3 1.0 copy-start.21
  158.3 1.3 copy-start.18
where the time goes:
time: 190 us; the launch traced here: 188 us
  waiting for transfers between devices  57 us (30%)
  Pallas kernels  48.3 us (25%)
  starting transfers between devices  47.8 us (25%)
  between operations  15.3 us (8%)
  other arithmetic  12.5 us (7%)
  local copies, waits for them, and re-layouts  6.02 us (3%)
    ppermute x8, waiting for transfers between devices, to_chip(): return lax.ppermute(value, 'shard', pairs)  52 us
    pallas_call x2, Pallas kernels, phase_call(): pl.pallas_call(functools.partial(phase_kernel, len(pieces), cut, wide, bl...  44 us
    ppermute x8, starting transfers between devices, to_chip(): return lax.ppermute(value, 'shard', pairs)  39.6 us
    ppermute x4, starting transfers between devices, to_slot(): return lax.ppermute(value, 'expert', [(i, i ^ bit) for i in range(n_slot)])  5.94 us
    ppermute x4, waiting for transfers between devices, to_slot(): return lax.ppermute(value, 'expert', [(i, i ^ bit) for i in range(n_slot)])  4.9 us
    pallas_call x1, Pallas kernels, hidden_transposed(): pl.pallas_call(hidden_kernel, grid=(rows // tall,), in_specs=[block, bloc...  4.35 us
  transfers between devices with their start and end apart: 21, of which 5 were waited for; matrix products, arithmetic and copies ran while one was open for 7% of the time, Pallas kernels for 14%

commit v1 on v0

--- a/solution.py
+++ b/solution.py
@@ -55,7 +55,7 @@
     gate_out[0] = (d_hidden * up * slope).astype(gate_out.dtype)
 
 
-def phase_kernel(n_pieces, layout, wide, blocks, grad_in, gates, update, flag_ref, *refs):
+def phase_kernel(n_pieces, layout, wide, blocks, tall, grad_in, gates, update, flag_ref, *refs):
     refs = list(refs)
     pieces = [refs.pop(0) for _ in range(n_pieces)]
     hidden_ref = refs.pop(0) if blocks else None
@@ -138,19 +138,20 @@
 
 
 def phase_call(flags, pieces, layout, hidden=None, master=None, grad=None, gate_up=None,
-               update=False, d_model=None):
+               update=False, d_model=None, tall=256):
     if master is not None:
         _, ffw, d_model = master.shape
     else:
         ffw = hidden.shape[0]
     rows = gate_up[0].shape[1] if hidden is None else hidden.shape[1]
-    wide = 512
+    wide = next(w for w in (1024, 768, 512, 128) if d_model % w == 0)
     blocks = d_model // wide if hidden is not None else 0
     lines = ffw // tall if master is not None else 0
     cut = []
     for ref, index, row, first, count in layout:
-        for at in range(0, count, wide):
-            cut.append((ref, index, row, at, first + at, wide))
+        piece = wide if blocks else count
+        for at in range(0, count, piece):
+            cut.append((ref, index, row, at, first + at, piece))
     row_block = lambda i: jnp.maximum(i - blocks, 0)
     col_block = lambda i: jnp.minimum(i, blocks - 1)
     anywhere = pl.BlockSpec(memory_space=pl.ANY)
@@ -164,7 +165,7 @@
         pltpu.SemaphoreType.DMA((len(cut),)),
     ]
     if hidden is not None:
-        specs.append(pl.BlockSpec((ffw, rows), lambda i, flag: (0, 0)))
+        specs.append(pl.BlockSpec((ffw, rows), lambda i, flag: (0, 0), pipeline_mode=pl.Buffered(1)))
         args.append(hidden)
     if master is not None:
         specs.append(anywhere)
@@ -189,7 +190,7 @@
     dots = (hidden is not None) + (gate_up is not None)
     return pl.pallas_call(
         functools.partial(
-            phase_kernel, len(pieces), cut, wide, blocks, grad is not None, gate_up is not None,
+            phase_kernel, len(pieces), cut, wide, blocks, tall, grad is not None, gate_up is not None,
             update,
         ),
         grid_spec=pltpu.PrefetchScalarGridSpec(
@@ -247,15 +248,23 @@
     def share(bit):
         return jnp.any(same & (order[:, None] == slot) & (order[None, :] == slot ^ bit))
 
+    orders = {}
+
+    def send(value, axis, pairs):
+        turn = orders.get((axis, *sorted(pairs)), 0)
+        orders[(axis, *sorted(pairs))] = turn + 1
+        turn, back = divmod(turn, 2)
+        pairs = pairs[turn:] + pairs[:turn]
+        return lax.ppermute(value, axis, pairs[::-1] if back else pairs)
+
     def to_slot(value, bit):
-        return lax.ppermute(value, "expert", [(i, i ^ bit) for i in range(n_slot)])
+        return send(value, "expert", [(i, i ^ bit) for i in range(n_slot)])
 
     def to_core(value):
-        return lax.ppermute(value, "shard", [(i, i ^ 1) for i in range(n_shard)])
+        return send(value, "shard", [(i, i ^ 1) for i in range(n_shard)])
 
     def to_chip(value, pairs):
-        pairs = [(2 * a + c, 2 * b + c) for a, b in pairs for c in range(2)]
-        return lax.ppermute(value, "shard", pairs)
+        return send(value, "shard", [(2 * a + c, 2 * b + c) for a, b in pairs for c in range(2)])
 
     def along_chips(block, held=None):
         if chips != 4:
@@ -291,6 +300,7 @@
         return jnp.concatenate(done)
 
     def body(mode, grad_out, gate_pre, up_pre, counts, placement, master):
+        orders.clear()
         live = jnp.arange(rows, dtype=jnp.int32) < counts[0, 0]
         masked = jnp.where(live[:, None], grad_out[0], jnp.zeros((), grad_out.dtype))
 
@@ -303,23 +313,24 @@
             early = to_slot(masked[:, :middle], 1)
             hidden = hidden_transposed(gate_pre, up_pre)
             high = hidden.shape[0] // 2
-            top = to_slot(after(hidden[:high], early), 1)
-            low = to_slot(after(hidden[high:], early), 1)
-            mine = along_chips(masked, top)
+            top = to_slot(hidden[:high], 1)
+            low = to_slot(hidden[high:], 1)
+            mine = along_chips(masked, (early, top))
             other = [to_core(piece) for piece in mine]
             first = along_chips(early)
-            first = first + [to_core(piece) for piece in first]
-            late = jnp.stack([piece[:, middle:] for piece in mine])
-            late = to_slot(after(late, low), 1)
-            late = [late, to_core(late)]
+            late = to_slot(jnp.stack([piece[:, middle:] for piece in mine]), 1)
             theirs = jnp.concatenate([top, low])
             steps = [(chip + far) % chips for far in range(chips)]
             spots = [(2 * s + (core ^ swap)) * rows for swap in range(2) for s in steps]
             flags = jnp.stack([share(1).astype(jnp.int32)] + spots)
             layout = [(i, None, (1 + i,), 0, d_model) for i in range(n_shard)]
             d_gate, d_up, grad = phase_call(
-                flags, after(mine, first[2]) + other, layout, hidden, master, gate_up=gate_up
+                flags, after(mine, (first[2], low)) + other, layout, hidden, master,
+                gate_up=gate_up, tall=512,
             )
+            held = after(first[1:] + [late], grad)
+            first = first + [to_core(piece) for piece in first[:1] + held[:-1]]
+            late = [late, to_core(held[-1])]
             layout = [(i, None, (1 + i,), 0, middle) for i in range(n_shard)]
             layout += [
                 (n_shard + i // chips, i % chips, (1 + i,), middle, d_model - middle)
@@ -353,7 +364,7 @@
                     grad = grad + jnp.where(share(bit), got, jnp.zeros((), got.dtype))
             grads.append(grad)
         layout = layout + [(1, None, 0, half, half)]
-        d_gate, d_up = phase_call(flags, [one, two], layout, master=master, gate_up=gate_up)
+        d_gate, d_up = phase_call(flags, [one, two], layout, master=master, gate_up=gate_up, tall=512)
         return d_gate, d_up, update_call(master, grads)
 
     modes = ["none", "pair", "four"] + (["mixed"] if n_slot > 4 else [])

time: 190 us -> 188 us (0.989)
  waiting for transfers between devices: 57 us -> 68.2 us
  starting transfers between devices: 47.8 us -> 38.9 us
  other arithmetic: 12.5 us -> 8.01 us
  local copies, waits for them, and re-layouts: 6.02 us -> 10 us
  Pallas kernels: 48.3 us -> 45.6 us
    ppermute x21, waiting for transfers between devices: 57 us -> 68.2 us  [send(): return lax.ppermute(value, axis, pairs[::-1] if back else pairs)]
    ppermute x21, starting transfers between devices: 47.8 us -> 38.9 us  [send(): return lax.ppermute(value, axis, pairs[::-1] if back else pairs)]
    cond x24 -> x46, local copies, waits for them, and re-layouts: 1.66 us -> 4.74 us
    pallas_call x2, Pallas kernels: 44 us -> 40.9 us  [phase_call(): pl.pallas_call(functools.partial(phase_kernel, len(pieces), cut, wide, bl...]
  transfers between devices with their start and end apart: 21 -> 21, of which waited for: 5 -> 12; matrix products, arithmetic and copies ran while one was open for 7% -> 4% of each run, Pallas kernels for 14% -> 12%
where the time goes in v1:
time: 188 us
  waiting for transfers between devices  68.2 us (36%)
  Pallas kernels  45.6 us (24%)
  starting transfers between devices  38.9 us (21%)
  between operations  15.3 us (8%)
  local copies, waits for them, and re-layouts  10 us (5%)
  other arithmetic  8.01 us (4%)
    ppermute x21, waiting for transfers between devices, send(): return lax.ppermute(value, axis, pairs[::-1] if back else pairs)  68.2 us
    pallas_call x2, Pallas kernels, phase_call(): pl.pallas_call(functools.partial(phase_kernel, len(pieces), cut, wide, bl...  40.9 us
    ppermute x21, starting transfers between devices, send(): return lax.ppermute(value, axis, pairs[::-1] if back else pairs)  38.9 us
    cond x46, local copies, waits for them, and re-layouts  4.74 us
    pallas_call x1, Pallas kernels, hidden_transposed(): pl.pallas_call(hidden_kernel, grid=(rows // tall,), in_specs=[block, bloc...  4.71 us
  transfers between devices with their start and end apart: 21, of which 12 were waited for; matrix products, arithmetic and copies ran while one was open for 4% of the time, Pallas kernels for 12%

profile of v1, /device:TPU:0, one launch (start us, length us, event | category | flops | bytes accessed | tf_op | source)
XLA Modules:
  0.0 187.6 jit_solution(12274952059846702608)
XLA Ops:
  7.2 0.8 broadcast_compare_fusion.2
  8.0 1.4 convert_reduce_fusion
  10.7 170.0 %conditional.1 = ((bf16[1,1024,1024]{2,1,0:T(8,128)(2,1)}, bf16[1,1024,1024]{2,1,0:T(8,128)(2,1)}, f32[1,1024,3072]{2,1,0:T(8,128)})) conditional(s32[]{:T(128)} %clamp.3, (s32[1,1]{1,0:T(1,128)}, bf16[1,128,3072]{2,1,0:T(8,128)(2,1)}, bf16[1,1024,1024]{2,1,0:T(8,128)(2,1)}, bf16[1,1024,1024]{2,1,0:T(8,128)(2,1)}, ...), branch_computations={%region_2.3_spmd, %region_3.5_spmd, %region_5.6_spmd} | conditional | flops 19334823936 | bytes 226756256 | solution.py:373
  10.8 4.7 %branch_1_fun.3.refs_8_ = bf16[1024,1024]{1,0:T(8,128)(2,1)} custom-call(bf16[1,1024,1024]{2,1,0:T(8,128)(2,1)} %get-tuple-element.56.gate_ref.refs_10_, bf16[1,1024,1024]{2,1,0:T(8,128)(2,1)} %get-tuple-element.57.up_ref.refs_11_), custom_call_target="tpu_custom_call" | custom-call | tf_op jit(solution)/shard_map/cond/branch_1_fun/pallas_call | solution.py:29
  15.5 2.8 %fusion.2 = (bf16[512,1024]{1,0:T(8,128)(2,1)}, bf16[512,1024]{1,0:T(8,128)(2,1)S(1)}) fusion(bf16[1024,1024]{1,0:T(8,128)(2,1)} %branch_1_fun.3.refs_8_), kind=kLoop, calls=%fused_computation.66 | loop fusion | bytes 4194304 | tf_op jit(solution)/shard_map/cond/branch_1_fun/slice | solution.py:317
  18.2 2.9 %collective-permute-start.2 = (bf16[512,1024]{1,0:T(8,128)(2,1)S(1)}, bf16[512,1024]{1,0:T(8,128)(2,1)S(1)}, u32[]{:S(2)}, u32[]{:S(2)}) collective-permute-start(bf16[512,1024]{1,0:T(8,128)(2,1)S(1)} %get-tuple-element.117), channel_id=1, source_target_pairs={{24,16},{16,24},{8,0},{0,8},{25,17},{17,25},{9,1},{1,9},{26,18},{1... | collective-permute-start | bytes 3145736 | tf_op jit(solution)/shard_map/cond/branch_1_fun/ppermute | solution.py:258
  21.2 0.6 iota_compare_fusion.1
  22.0 2.7 %collective-permute-start = (bf16[128,3072]{1,0:T(8,128)(2,1)S(1)}, bf16[128,3072]{1,0:T(8,128)(2,1)}, u32[]{:S(2)}, u32[]{:S(2)}) collective-permute-start(bf16[128,3072]{1,0:T(8,128)(2,1)S(1)} %bitcast_select_fusion.1.refs_0_), channel_id=1, source_target_pairs={{0,4},{1,5},{2,6},{3,7},{4,0},{5,1},{6,2},{7,3},{8,12},{9,13},{10,... | collective-permute-start | bytes 2359304 | tf_op jit(solution)/shard_map/cond/branch_1_fun/ppermute | solution.py:258
  24.6 0.8 slice.39
  25.4 0.5 collective-permute-start.1
  26.0 4.5 %collective-permute-start.5 = (bf16[128,3072]{1,0:T(8,128)(2,1)S(1)}, bf16[128,3072]{1,0:T(8,128)(2,1)}, u32[]{:S(2)}, u32[]{:S(2)}) collective-permute-start(bf16[128,3072]{1,0:T(8,128)(2,1)S(1)} %bitcast_select_fusion.1.refs_0_), channel_id=1, source_target_pairs={{0,2},{1,3},{2,4},{3,5},{4,6},{5,7},{8,10},{9,11},{10,12},{11,13},... | collective-permute-start | bytes 2359304 | tf_op jit(solution)/shard_map/cond/branch_1_fun/ppermute | solution.py:258
  30.4 25.1 %collective-permute-done.1.refs_0_ = bf16[128,2048]{1,0:T(8,128)(2,1)S(1)} collective-permute-done((bf16[128,2048]{1,0:T(8,128)(2,1)}, bf16[128,2048]{1,0:T(8,128)(2,1)S(1)}, u32[]{:S(2)}, u32[]{:S(2)}) %collective-permute-start.1) | collective-permute-done | bytes 524320 | tf_op jit(solution)/shard_map/cond/branch_1_fun/ppermute | solution.py:258
  55.5 1.3 collective-permute-start.4
  56.8 2.0 %collective-permute-done.refs_2_ = bf16[128,3072]{1,0:T(8,128)(2,1)} collective-permute-done((bf16[128,3072]{1,0:T(8,128)(2,1)S(1)}, bf16[128,3072]{1,0:T(8,128)(2,1)}, u32[]{:S(2)}, u32[]{:S(2)}) %collective-permute-start) | collective-permute-done | bytes 786464 | tf_op jit(solution)/shard_map/cond/branch_1_fun/ppermute | solution.py:258
  58.9 1.3 collective-permute-start.3
  60.2 5.1 %collective-permute-start.6 = (bf16[128,2048]{1,0:T(8,128)(2,1)S(1)}, bf16[128,2048]{1,0:T(8,128)(2,1)}, u32[]{:S(2)}, u32[]{:S(2)}) collective-permute-start(bf16[128,2048]{1,0:T(8,128)(2,1)S(1)} %collective-permute-done.1.refs_0_), channel_id=1, source_target_pairs={{7,3},{6,2},{5,1},{4,0},{3,7},{2,6},{1,5},{0,4},{15,11},{14,10},{1... | collective-permute-start | bytes 1572872 | tf_op jit(solution)/shard_map/cond/branch_1_fun/ppermute | solution.py:258
  65.3 0.7 and_reduce_fusion
  66.6 0.7 stack.42.flag_ref
  67.3 1.0 slice_bitcast_fusion.1
  68.3 1.6 collective-permute-start.7
  69.8 9.3 %collective-permute-done.4 = bf16[128,3072]{1,0:T(8,128)(2,1)} collective-permute-done((bf16[128,3072]{1,0:T(8,128)(2,1)S(1)}, bf16[128,3072]{1,0:T(8,128)(2,1)}, u32[]{:S(2)}, u32[]{:S(2)}) %collective-permute-start.4) | collective-permute-done | bytes 786464 | tf_op jit(solution)/shard_map/cond/branch_1_fun/ppermute | solution.py:258
  79.2 13.8 %collective-permute-start.14 = (bf16[128,2048]{1,0:T(8,128)(2,1)S(1)}, bf16[128,2048]{1,0:T(8,128)(2,1)S(1)}, u32[]{:S(2)}, u32[]{:S(2)}) collective-permute-start(bf16[128,2048]{1,0:T(8,128)(2,1)S(1)} %collective-permute-done.1.refs_0_), channel_id=1, source_target_pairs={{5,7},{4,6},{3,5},{2,4},{1,3},{0,2},{13,15},{12,14},{11,13},{10,12... | collective-permute-start | bytes 1572872 | tf_op jit(solution)/shard_map/cond/branch_1_fun/ppermute | solution.py:258
  93.0 6.9 %collective-permute-done.6.refs_2_ = bf16[128,2048]{1,0:T(8,128)(2,1)} collective-permute-done((bf16[128,2048]{1,0:T(8,128)(2,1)S(1)}, bf16[128,2048]{1,0:T(8,128)(2,1)}, u32[]{:S(2)}, u32[]{:S(2)}) %collective-permute-start.6) | collective-permute-done | bytes 524320 | tf_op jit(solution)/shard_map/cond/branch_1_fun/ppermute | solution.py:258
  99.9 1.3 collective-permute-start.13
  101.2 4.8 %collective-permute-done.3 = bf16[128,3072]{1,0:T(8,128)(2,1)S(1)} collective-permute-done((bf16[128,3072]{1,0:T(8,128)(2,1)}, bf16[128,3072]{1,0:T(8,128)(2,1)S(1)}, u32[]{:S(2)}, u32[]{:S(2)}) %collective-permute-start.3) | collective-permute-done | bytes 786464 | tf_op jit(solution)/shard_map/cond/branch_1_fun/ppermute | solution.py:258
  106.0 0.9 copy-done.23
  106.9 1.5 collective-permute-start.12
  108.4 1.5 broadcast_select_fusion
  110.0 7.3 %collective-permute-done.13 = bf16[128,2048]{1,0:T(8,128)(2,1)S(1)} collective-permute-done((bf16[128,2048]{1,0:T(8,128)(2,1)S(1)}, bf16[128,2048]{1,0:T(8,128)(2,1)S(1)}, u32[]{:S(2)}, u32[]{:S(2)}) %collective-permute-start.13) | collective-permute-done | bytes 524320 | tf_op jit(solution)/shard_map/cond/branch_1_fun/ppermute | solution.py:258
  117.2 9.6 %collective-permute-done.12 = bf16[128,2048]{1,0:T(8,128)(2,1)S(1)} collective-permute-done((bf16[128,2048]{1,0:T(8,128)(2,1)}, bf16[128,2048]{1,0:T(8,128)(2,1)S(1)}, u32[]{:S(2)}, u32[]{:S(2)}) %collective-permute-start.12) | collective-permute-done | bytes 524320 | tf_op jit(solution)/shard_map/cond/branch_1_fun/ppermute | solution.py:258
  127.0 1.1 pad_maximum_fusion.1
  128.1 1.4 collective-permute-start.16
  129.6 0.8 copy-done.30
  130.5 0.3 copy-done.31
  130.7 0.9 copy-done.32
  131.7 22.1 %branch_1_fun.4 = (bf16[1,1024,1024]{2,1,0:T(8,128)(2,1)}, bf16[1,1024,1024]{2,1,0:T(8,128)(2,1)}, bf16[1024,3072]{1,0:T(8,128)(2,1)}) custom-call(s32[9]{0:T(128)} %stack.42.flag_ref, bf16[128,3072]{1,0:T(8,128)(2,1)} %copy-done.10, bf16[128,3072]{1,0:T(8,128)(2,1)} %copy-done.17, bf16[128,3072]{1,0:T(8,128)(2,1)} %collective-permute-done.refs_2_, ...), custom_call_target="tpu_custom_call" | custom-call | flops 12884901888 | bytes 25165824 | tf_op jit(solution)/shard_map/cond/branch_1_fun/pallas_call | solution.py:191
  153.8 0.2 collective-permute-done.16.refs_8_
  154.1 0.4 collective-permute-start.15
  154.6 0.4 collective-permute-start.18
  155.1 1.6 pad_maximum_fusion.refs_10_
  156.7 1.2 collective-permute-done.15.refs_4_
  157.9 1.0 collective-permute-done.17.refs_5_
  158.9 0.2 collective-permute-done.18.refs_6_
  159.1 0.6 collective-permute-done.19.refs_7_
  159.8 0.2 copy-done.28
  160.0 0.5 copy-done.29
  160.5 1.0 copy-done.22
  161.5 18.8 %branch_1_fun.5 = f32[1,1024,3072]{2,1,0:T(8,128)} custom-call(s32[9]{0:T(128)} %stack.42.flag_ref, bf16[128,2048]{1,0:T(8,128)(2,1)} %copy-done.24, bf16[128,2048]{1,0:T(8,128)(2,1)} %copy-done.14, bf16[128,2048]{1,0:T(8,128)(2,1)} %collective-permute-done.6.refs_2_, bf16[128,2048]{1,0:T(8,128)(2,1)} %copy-done.13, bf16[128,2048]{1,0:T(8,128)(2,1)} %copy-done.26, ...), custom_call_target="tpu_custom_call" | custom-call | flops 6442450944 | bytes 25165824 | tf_op jit(solution)/shard_map/cond/branch_1_fun/pallas_call | solution.py:191
  (62 shorter events, 0.8 us)
Async XLA Ops:
  15.5 6.4 %copy-start.5 = (bf16[1,128,3072]{2,1,0:T(8,128)(2,1)S(1)}, bf16[1,128,3072]{2,1,0:T(8,128)(2,1)}, u32[]{:S(2)}) copy-start(bf16[1,128,3072]{2,1,0:T(8,128)(2,1)} %get-tuple-element.55) | copy-start | bytes 2359300 | tf_op jit(solution)/shard_map/cond
  18.2 40.7 %collective-permute-start.2 = (bf16[512,1024]{1,0:T(8,128)(2,1)S(1)}, bf16[512,1024]{1,0:T(8,128)(2,1)S(1)}, u32[]{:S(2)}, u32[]{:S(2)}) collective-permute-start(bf16[512,1024]{1,0:T(8,128)(2,1)S(1)} %get-tuple-element.117), channel_id=1, source_target_pairs={{24,16},{16,24},{8,0},{0,8},{25,17},{17,25},{9,1},{1,9},{26,18},{1... | collective-permute-start | bytes 3145736 | tf_op jit(solution)/shard_map/cond/branch_1_fun/ppermute | solution.py:258
  22.0 87.9 %copy-start.10 = (bf16[128,3072]{1,0:T(8,128)(2,1)}, bf16[128,3072]{1,0:T(8,128)(2,1)S(1)}, u32[]{:S(2)}) copy-start(bf16[128,3072]{1,0:T(8,128)(2,1)S(1)} %bitcast_select_fusion.1.refs_0_) | copy-start | bytes 2359300 | tf_op jit(solution)/shard_map/cond
  22.0 36.9 %collective-permute-start = (bf16[128,3072]{1,0:T(8,128)(2,1)S(1)}, bf16[128,3072]{1,0:T(8,128)(2,1)}, u32[]{:S(2)}, u32[]{:S(2)}) collective-permute-start(bf16[128,3072]{1,0:T(8,128)(2,1)S(1)} %bitcast_select_fusion.1.refs_0_), channel_id=1, source_target_pairs={{0,4},{1,5},{2,6},{3,7},{4,0},{5,1},{6,2},{7,3},{8,12},{9,13},{10,... | collective-permute-start | bytes 2359304 | tf_op jit(solution)/shard_map/cond/branch_1_fun/ppermute | solution.py:258
  25.4 30.1 %collective-permute-start.1 = (bf16[128,2048]{1,0:T(8,128)(2,1)}, bf16[128,2048]{1,0:T(8,128)(2,1)S(1)}, u32[]{:S(2)}, u32[]{:S(2)}) collective-permute-start(bf16[128,2048]{1,0:T(8,128)(2,1)} %slice.39), channel_id=1, source_target_pairs={{0,8},{8,0},{16,24},{24,16},{1,9},{9,1},{17,25},{25,17},{2,10},{10... | collective-permute-start | bytes 1572872 | tf_op jit(solution)/shard_map/cond/branch_1_fun/ppermute | solution.py:258
  26.0 103.6 %collective-permute-start.8 = (bf16[128,3072]{1,0:T(8,128)(2,1)S(1)}, bf16[128,3072]{1,0:T(8,128)(2,1)}, u32[]{:S(2)}, u32[]{:S(2)}) collective-permute-start(bf16[128,3072]{1,0:T(8,128)(2,1)S(1)} %bitcast_select_fusion.1.refs_0_), channel_id=1, source_target_pairs={{0,1},{1,0},{2,3},{3,2},{4,5},{5,4},{6,7},{7,6},{8,9},{9,8},{10,11... | collective-permute-start | bytes 2359304 | tf_op jit(solution)/shard_map/cond/branch_1_fun/ppermute | solution.py:258
  26.0 42.3 %collective-permute-start.5 = (bf16[128,3072]{1,0:T(8,128)(2,1)S(1)}, bf16[128,3072]{1,0:T(8,128)(2,1)}, u32[]{:S(2)}, u32[]{:S(2)}) collective-permute-start(bf16[128,3072]{1,0:T(8,128)(2,1)S(1)} %bitcast_select_fusion.1.refs_0_), channel_id=1, source_target_pairs={{0,2},{1,3},{2,4},{3,5},{4,6},{5,7},{8,10},{9,11},{10,12},{11,13},... | collective-permute-start | bytes 2359304 | tf_op jit(solution)/shard_map/cond/branch_1_fun/ppermute | solution.py:258
  55.5 74.1 %copy-start.24 = (bf16[128,2048]{1,0:T(8,128)(2,1)}, bf16[128,2048]{1,0:T(8,128)(2,1)S(1)}, u32[]{:S(2)}) copy-start(bf16[128,2048]{1,0:T(8,128)(2,1)S(1)} %collective-permute-done.1.refs_0_) | copy-start | bytes 1572868 | tf_op jit(solution)/shard_map/cond
  55.5 23.6 %collective-permute-start.4 = (bf16[128,3072]{1,0:T(8,128)(2,1)S(1)}, bf16[128,3072]{1,0:T(8,128)(2,1)}, u32[]{:S(2)}, u32[]{:S(2)}) collective-permute-start(bf16[128,3072]{1,0:T(8,128)(2,1)S(1)} %bitcast_select_fusion.1.refs_0_), channel_id=1, source_target_pairs={{2,0},{3,1},{4,2},{5,3},{6,4},{7,5},{10,8},{11,9},{12,10},{13,11},... | collective-permute-start | bytes 2359304 | tf_op jit(solution)/shard_map/cond/branch_1_fun/ppermute | solution.py:258
  58.9 47.1 %copy-start.18 = (bf16[512,1024]{1,0:T(8,128)(2,1)}, bf16[512,1024]{1,0:T(8,128)(2,1)S(1)}, u32[]{:S(2)}) copy-start(bf16[512,1024]{1,0:T(8,128)(2,1)S(1)} %collective-permute-done.2) | copy-start | bytes 3145732 | tf_op jit(solution)/shard_map/cond
  58.9 47.1 %collective-permute-start.3 = (bf16[128,3072]{1,0:T(8,128)(2,1)}, bf16[128,3072]{1,0:T(8,128)(2,1)S(1)}, u32[]{:S(2)}, u32[]{:S(2)}) collective-permute-start(bf16[128,3072]{1,0:T(8,128)(2,1)} %collective-permute-done.refs_2_), channel_id=1, source_target_pairs={{4,6},{5,7},{2,0},{3,1},{12,14},{13,15},{10,8},{11,9},{20,22},{21,... | collective-permute-start | bytes 2359304 | tf_op jit(solution)/shard_map/cond/branch_1_fun/ppermute | solution.py:258
  60.2 39.7 %collective-permute-start.6 = (bf16[128,2048]{1,0:T(8,128)(2,1)S(1)}, bf16[128,2048]{1,0:T(8,128)(2,1)}, u32[]{:S(2)}, u32[]{:S(2)}) collective-permute-start(bf16[128,2048]{1,0:T(8,128)(2,1)S(1)} %collective-permute-done.1.refs_0_), channel_id=1, source_target_pairs={{7,3},{6,2},{5,1},{4,0},{3,7},{2,6},{1,5},{0,4},{15,11},{14,10},{1... | collective-permute-start | bytes 1572872 | tf_op jit(solution)/shard_map/cond/branch_1_fun/ppermute | solution.py:258
  68.3 58.7 %collective-permute-start.7 = (bf16[512,1024]{1,0:T(8,128)(2,1)}, bf16[512,1024]{1,0:T(8,128)(2,1)S(1)}, u32[]{:S(2)}, u32[]{:S(2)}) collective-permute-start(bf16[512,1024]{1,0:T(8,128)(2,1)} %get-tuple-element.116), channel_id=1, source_target_pairs={{8,0},{16,24},{24,16},{0,8},{9,1},{17,25},{25,17},{1,9},{10,2},{18... | collective-permute-start | bytes 3145736 | tf_op jit(solution)/shard_map/cond/branch_1_fun/ppermute | solution.py:258
  79.2 30.7 %collective-permute-start.14 = (bf16[128,2048]{1,0:T(8,128)(2,1)S(1)}, bf16[128,2048]{1,0:T(8,128)(2,1)S(1)}, u32[]{:S(2)}, u32[]{:S(2)}) collective-permute-start(bf16[128,2048]{1,0:T(8,128)(2,1)S(1)} %collective-permute-done.1.refs_0_), channel_id=1, source_target_pairs={{5,7},{4,6},{3,5},{2,4},{1,3},{0,2},{13,15},{12,14},{11,13},{10,12... | collective-permute-start | bytes 1572872 | tf_op jit(solution)/shard_map/cond/branch_1_fun/ppermute | solution.py:258
  99.9 17.3 %collective-permute-start.13 = (bf16[128,2048]{1,0:T(8,128)(2,1)S(1)}, bf16[128,2048]{1,0:T(8,128)(2,1)S(1)}, u32[]{:S(2)}, u32[]{:S(2)}) collective-permute-start(bf16[128,2048]{1,0:T(8,128)(2,1)S(1)} %collective-permute-done.1.refs_0_), channel_id=1, source_target_pairs={{7,5},{6,4},{5,3},{4,2},{3,1},{2,0},{15,13},{14,12},{13,11},{12,10... | collective-permute-start | bytes 1572872 | tf_op jit(solution)/shard_map/cond/branch_1_fun/ppermute | solution.py:258
  106.0 0.9 copy-start.23
  106.9 19.9 %collective-permute-start.12 = (bf16[128,2048]{1,0:T(8,128)(2,1)}, bf16[128,2048]{1,0:T(8,128)(2,1)S(1)}, u32[]{:S(2)}, u32[]{:S(2)}) collective-permute-start(bf16[128,2048]{1,0:T(8,128)(2,1)} %collective-permute-done.6.refs_2_), channel_id=1, source_target_pairs={{3,1},{2,0},{5,7},{4,6},{11,9},{10,8},{13,15},{12,14},{19,17},{18,... | collective-permute-start | bytes 1572872 | tf_op jit(solution)/shard_map/cond/branch_1_fun/ppermute | solution.py:258
  109.9 18.3 %copy-start.16 = (bf16[128,3072]{1,0:T(8,128)(2,1)}, bf16[128,3072]{1,0:T(8,128)(2,1)S(1)}, u32[]{:S(2)}) copy-start(bf16[128,3072]{1,0:T(8,128)(2,1)S(1)} %get-tuple-element.62.refs_3_) | copy-start | bytes 2359300 | tf_op jit(solution)/shard_map/cond
  109.9 18.3 %copy-start.17 = (bf16[128,3072]{1,0:T(8,128)(2,1)}, bf16[128,3072]{1,0:T(8,128)(2,1)S(1)}, u32[]{:S(2)}) copy-start(bf16[128,3072]{1,0:T(8,128)(2,1)S(1)} %get-tuple-element.60.refs_1_) | copy-start | bytes 2359300 | tf_op jit(solution)/shard_map/cond
  109.9 19.7 %collective-permute-start.10 = (bf16[128,3072]{1,0:T(8,128)(2,1)}, bf16[128,3072]{1,0:T(8,128)(2,1)S(1)}, u32[]{:S(2)}, u32[]{:S(2)}) collective-permute-start(bf16[128,3072]{1,0:T(8,128)(2,1)} %collective-permute-done.refs_2_), channel_id=1, source_target_pairs={{1,0},{2,3},{3,2},{4,5},{5,4},{6,7},{7,6},{0,1},{9,8},{10,11},{11,... | collective-permute-start | bytes 2359304 | tf_op jit(solution)/shard_map/cond/branch_1_fun/ppermute | solution.py:258
  117.2 12.3 %collective-permute-start.11 = (bf16[128,3072]{1,0:T(8,128)(2,1)S(1)}, bf16[128,3072]{1,0:T(8,128)(2,1)S(1)}, u32[]{:S(2)}, u32[]{:S(2)}) collective-permute-start(bf16[128,3072]{1,0:T(8,128)(2,1)S(1)} %get-tuple-element.62.refs_3_), channel_id=1, source_target_pairs={{0,1},{7,6},{6,7},{5,4},{4,5},{3,2},{2,3},{1,0},{8,9},{15,14},{14,... | collective-permute-start | bytes 2359304 | tf_op jit(solution)/shard_map/cond/branch_1_fun/ppermute | solution.py:258
  126.8 2.8 %collective-permute-start.9 = (bf16[128,3072]{1,0:T(8,128)(2,1)S(1)}, bf16[128,3072]{1,0:T(8,128)(2,1)S(1)}, u32[]{:S(2)}, u32[]{:S(2)}) collective-permute-start(bf16[128,3072]{1,0:T(8,128)(2,1)S(1)} %get-tuple-element.60.refs_1_), channel_id=1, source_target_pairs={{7,6},{6,7},{5,4},{4,5},{3,2},{2,3},{1,0},{0,1},{15,14},{14,15},{1... | collective-permute-start | bytes 2359304 | tf_op jit(solution)/shard_map/cond/branch_1_fun/ppermute | solution.py:258
  126.8 4.8 %copy-start.3 = (bf16[1,1024,1024]{2,1,0:T(8,128)(2,1)S(1)}, bf16[1,1024,1024]{2,1,0:T(8,128)(2,1)}, u32[]{:S(2)}) copy-start(bf16[1,1024,1024]{2,1,0:T(8,128)(2,1)} %get-tuple-element.57.up_ref.refs_11_) | copy-start | bytes 6291460 | tf_op jit(solution)/shard_map/cond
  126.9 27.6 %copy-start.14 = (bf16[128,2048]{1,0:T(8,128)(2,1)}, bf16[128,2048]{1,0:T(8,128)(2,1)S(1)}, u32[]{:S(2)}) copy-start(bf16[128,2048]{1,0:T(8,128)(2,1)S(1)} %get-tuple-element.67.refs_1_) | copy-start | bytes 1572868 | tf_op jit(solution)/shard_map/cond
  126.9 28.1 %copy-start.13 = (bf16[128,2048]{1,0:T(8,128)(2,1)}, bf16[128,2048]{1,0:T(8,128)(2,1)S(1)}, u32[]{:S(2)}) copy-start(bf16[128,2048]{1,0:T(8,128)(2,1)S(1)} %get-tuple-element.69.refs_3_) | copy-start | bytes 1572868 | tf_op jit(solution)/shard_map/cond
  126.9 4.7 %copy-start.1 = (bf16[1,1024,1024]{2,1,0:T(8,128)(2,1)S(1)}, bf16[1,1024,1024]{2,1,0:T(8,128)(2,1)}, u32[]{:S(2)}) copy-start(bf16[1,1024,1024]{2,1,0:T(8,128)(2,1)} %get-tuple-element.56.gate_ref.refs_10_) | copy-start | bytes 6291460 | tf_op jit(solution)/shard_map/cond
  127.0 2.7 %copy-start.20 = (bf16[512,1024]{1,0:T(8,128)(2,1)}, bf16[512,1024]{1,0:T(8,128)(2,1)S(1)}, u32[]{:S(2)}) copy-start(bf16[512,1024]{1,0:T(8,128)(2,1)S(1)} %collective-permute-done.7) | copy-start | bytes 3145732 | tf_op jit(solution)/shard_map/cond
  128.1 25.9 %collective-permute-start.16 = (bf16[4,128,1024]{2,1,0:T(8,128)(2,1)}, bf16[4,128,1024]{2,1,0:T(8,128)(2,1)}, u32[]{:S(2)}, u32[]{:S(2)}) collective-permute-start(bf16[4,128,1024]{2,1,0:T(8,128)(2,1)} %pad_maximum_fusion.1), channel_id=1, source_target_pairs={{0,8},{24,16},{16,24},{8,0},{1,9},{25,17},{17,25},{9,1},{2,10},{26... | collective-permute-start | bytes 3145736 | tf_op jit(solution)/shard_map/cond/branch_1_fun/ppermute | solution.py:258
  129.6 0.9 copy-start.30
  129.6 1.1 copy-start.31
  130.7 0.9 copy-start.32
  131.7 22.4 %copy-start.25 = (bf16[128,2048]{1,0:T(8,128)(2,1)S(1)}, bf16[128,2048]{1,0:T(8,128)(2,1)}, u32[]{:S(2)}) copy-start(bf16[128,2048]{1,0:T(8,128)(2,1)} %copy-done.24) | copy-start | bytes 1572868 | tf_op jit(solution)/shard_map/cond
  131.7 23.5 %copy-start.19 = (bf16[512,1024]{1,0:T(8,128)(2,1)S(1)}, bf16[512,1024]{1,0:T(8,128)(2,1)}, u32[]{:S(2)}) copy-start(bf16[512,1024]{1,0:T(8,128)(2,1)} %copy-done.18) | copy-start | bytes 3145732 | tf_op jit(solution)/shard_map/cond
  131.7 23.5 %copy-start.21 = (bf16[512,1024]{1,0:T(8,128)(2,1)S(1)}, bf16[512,1024]{1,0:T(8,128)(2,1)}, u32[]{:S(2)}) copy-start(bf16[512,1024]{1,0:T(8,128)(2,1)} %copy-done.20) | copy-start | bytes 3145732 | tf_op jit(solution)/shard_map/cond
  154.0 5.7 %collective-permute-start.20 = (bf16[4,128,1024]{2,1,0:T(8,128)(2,1)}, bf16[4,128,1024]{2,1,0:T(8,128)(2,1)S(1)}, u32[]{:S(2)}, u32[]{:S(2)}) collective-permute-start(bf16[4,128,1024]{2,1,0:T(8,128)(2,1)} %collective-permute-done.16.refs_8_), channel_id=1, source_target_pairs={{4,5},{5,4},{6,7},{7,6},{0,1},{1,0},{2,3},{3,2},{12,13},{13,12},{1... | collective-permute-start | bytes 3145736 | tf_op jit(solution)/shard_map/cond/branch_1_fun/ppermute | solution.py:258
  154.1 3.8 %collective-permute-start.15 = (bf16[128,2048]{1,0:T(8,128)(2,1)S(1)}, bf16[128,2048]{1,0:T(8,128)(2,1)S(1)}, u32[]{:S(2)}, u32[]{:S(2)}) collective-permute-start(bf16[128,2048]{1,0:T(8,128)(2,1)S(1)} %copy-done.25), channel_id=1, source_target_pairs={{2,3},{3,2},{4,5},{5,4},{6,7},{7,6},{0,1},{1,0},{10,11},{11,10},{1... | collective-permute-start | bytes 1572872 | tf_op jit(solution)/shard_map/cond/branch_1_fun/ppermute | solution.py:258
  154.5 4.4 %collective-permute-start.17 = (bf16[128,2048]{1,0:T(8,128)(2,1)S(1)}, bf16[128,2048]{1,0:T(8,128)(2,1)S(1)}, u32[]{:S(2)}, u32[]{:S(2)}) collective-permute-start(bf16[128,2048]{1,0:T(8,128)(2,1)S(1)} %get-tuple-element.67.refs_1_), channel_id=1, source_target_pairs={{1,0},{0,1},{7,6},{6,7},{5,4},{4,5},{3,2},{2,3},{9,8},{8,9},{15,14... | collective-permute-start | bytes 1572872 | tf_op jit(solution)/shard_map/cond/branch_1_fun/ppermute | solution.py:258
  154.6 4.5 %collective-permute-start.18 = (bf16[128,2048]{1,0:T(8,128)(2,1)}, bf16[128,2048]{1,0:T(8,128)(2,1)S(1)}, u32[]{:S(2)}, u32[]{:S(2)}) collective-permute-start(bf16[128,2048]{1,0:T(8,128)(2,1)} %collective-permute-done.6.refs_2_), channel_id=1, source_target_pairs={{3,2},{4,5},{5,4},{6,7},{7,6},{0,1},{1,0},{2,3},{11,10},{12,13},{1... | collective-permute-start | bytes 1572872 | tf_op jit(solution)/shard_map/cond/branch_1_fun/ppermute | solution.py:258
  155.1 4.6 %collective-permute-start.19 = (bf16[128,2048]{1,0:T(8,128)(2,1)S(1)}, bf16[128,2048]{1,0:T(8,128)(2,1)S(1)}, u32[]{:S(2)}, u32[]{:S(2)}) collective-permute-start(bf16[128,2048]{1,0:T(8,128)(2,1)S(1)} %get-tuple-element.69.refs_3_), channel_id=1, source_target_pairs={{2,3},{1,0},{0,1},{7,6},{6,7},{5,4},{4,5},{3,2},{10,11},{9,8},{8,9... | collective-permute-start | bytes 1572872 | tf_op jit(solution)/shard_map/cond/branch_1_fun/ppermute | solution.py:258
  157.9 1.8 copy-start.26
  158.9 0.8 copy-start.27
  159.1 0.9 copy-start.28
  159.7 0.8 copy-start.29
  160.5 1.0 copy-start.22
